TPU v7x, 256 devices: a whole 4x4x8 slice. The times are simulated.
256 devices in a mesh: group: 32 (over z, x_lo, core), tensor: 8 (over y, x_hi).
Axes of the slice: x: 4 (x_hi: 2, x_lo: 2; x = x_hi * 2 + x_lo), y: 4, z: 8, core: 2. Of those that a mesh axis runs over, the one named last changes fastest.
Arguments:
- queries: bfloat16 [4, 4096, 8192], P(None, 'group', 'tensor'), may hold values from -80 to 80
- step_key_rows: bfloat16 [4, 4096, 1024], P(None, 'group', 'tensor'), may hold values from -6 to 6
- step_value_rows: bfloat16 [4, 4096, 1024], P(None, 'group', 'tensor'), may hold values from -6 to 6
- cached_key_rows: bfloat16 [4096, 32, 1024], P('group', None, 'tensor'), may hold values from -5 to 5
- cached_value_rows: bfloat16 [4096, 32, 1024], P('group', None, 'tensor'), may hold values from -6 to 6
- lengths: int32 [4096], P('group'), may hold values from 2 to 32, as said below
- output_weight: bfloat16 [8192, 4096], P('tensor'), may hold values from -0.0625 to 0.0625
- down_factor: float32 [8192, 64], P('group'), may hold values from -0.0625 to 0.0625
- up_factor: float32 [64, 4096], P(None, 'group'), may hold values from -0.75 to 0.75
Outputs:
- attended: bfloat16 [4, 4096, 4096], P(None, 'group', 'tensor')
Inputs may be any that keep to these rules, and one draw needn't show every extreme that they name: `lengths`: some row holds all 32 positions.
All inputs are finite; a program needn't handle non-finite values.
Results may differ from a plain program's by a relative error of at most 0.02.
Values may be sent and summed in bfloat16 or wider, within the bound.
A program may use at most 128 MiB of HBM per device.

v0:
```python
import math

import jax
import jax.numpy as jnp
from jax import lax
from jax.sharding import PartitionSpec as P

QUERY_HEADS = 64
KVH = 8
HEAD_SIZE = 128


adapter_scale = 2.0


def attend(query, cache_k, cache_v, fresh_k, fresh_v, lengths):
    row_count = query.shape[0]
    kv_heads = cache_k.shape[2] // HEAD_SIZE
    group_size = QUERY_HEADS // KVH
    cache_len = cache_k.shape[1]
    query_h = query.reshape(row_count, kv_heads, group_size, HEAD_SIZE)
    keys_c = cache_k.reshape(row_count, cache_len, kv_heads, HEAD_SIZE)
    values_c = cache_v.reshape(row_count, cache_len, kv_heads, HEAD_SIZE)
    keys_n = fresh_k.reshape(fresh_k.shape[0], row_count, kv_heads, HEAD_SIZE)
    values_n = fresh_v.reshape(fresh_v.shape[0], row_count, kv_heads, HEAD_SIZE)
    inverse_root = 1.0 / math.sqrt(HEAD_SIZE)
    cache_scores = (
        jnp.einsum("rkgd,rckd->rkgc", query_h, keys_c, preferred_element_type=jnp.float32)
        * inverse_root
    )
    in_cache = lax.broadcasted_iota(jnp.int32, (row_count, 1, 1, cache_len), 3) < lengths.reshape(
        row_count, 1, 1, 1
    )
    cache_scores = jnp.where(in_cache, cache_scores, -jnp.inf)
    fresh_scores = (
        jnp.einsum("rkgd,trkd->rkgt", query_h, keys_n, preferred_element_type=jnp.float32)
        * inverse_root
    )
    row_max = jnp.maximum(
        jnp.max(cache_scores, axis=-1, keepdims=True), jnp.max(fresh_scores, axis=-1, keepdims=True)
    )
    cache_exp = jnp.exp(cache_scores - row_max)
    fresh_exp = jnp.exp(fresh_scores - row_max)
    denominator = jnp.sum(cache_exp, axis=-1, keepdims=True) + jnp.sum(
        fresh_exp, axis=-1, keepdims=True
    )
    cache_weights = (cache_exp / denominator).astype(jnp.bfloat16)
    fresh_weights = (fresh_exp / denominator).astype(jnp.bfloat16)
    attention_context = jnp.einsum(
        "rkgc,rckd->rkgd", cache_weights, values_c, preferred_element_type=jnp.float32
    )
    attention_context = attention_context + jnp.einsum(
        "rkgt,trkd->rkgd", fresh_weights, values_n, preferred_element_type=jnp.float32
    )
    return attention_context.reshape(row_count, kv_heads * group_size * HEAD_SIZE).astype(
        jnp.bfloat16
    )


def body(
    queries,
    step_key_rows,
    step_value_rows,
    cached_key_rows,
    cached_value_rows,
    lengths,
    output_weight,
    down_factor,
    up_factor,
):
    tensor_pos = lax.axis_index("tensor")
    tensor_count = lax.axis_size("tensor")
    gathered_down_factor = lax.all_gather(
        down_factor.astype(jnp.bfloat16), "group", axis=0, tiled=True
    ).astype(down_factor.dtype)
    gathered_up_factor = lax.all_gather(
        up_factor.astype(jnp.bfloat16), "group", axis=1, tiled=True
    ).astype(up_factor.dtype)
    steps_count = queries.shape[0]
    contexts = []
    for step_index in range(steps_count):
        contexts.append(
            attend(
                queries[step_index],
                cached_key_rows,
                cached_value_rows,
                step_key_rows[: step_index + 1],
                step_value_rows[: step_index + 1],
                lengths,
            )
        )
    attention_context = jnp.stack(contexts)
    head_width = attention_context.shape[2]
    columns = output_weight.shape[1] // tensor_count
    partial_term = jnp.einsum(
        "srw,wd->srd", attention_context, output_weight, preferred_element_type=jnp.float32
    )
    base_sum = lax.psum_scatter(
        partial_term.astype(jnp.bfloat16), "tensor", scatter_dimension=2, tiled=True
    ).astype(jnp.float32)
    local_a = lax.dynamic_slice_in_dim(gathered_down_factor, tensor_pos * head_width, head_width, 0)
    local_proj = jnp.einsum(
        "srw,wk->srk",
        attention_context.astype(jnp.float32),
        local_a,
        precision=lax.Precision.HIGHEST,
    )
    rank_projected = lax.psum(local_proj.astype(jnp.bfloat16), "tensor").astype(jnp.float32)
    local_b = lax.dynamic_slice_in_dim(gathered_up_factor, tensor_pos * columns, columns, 1)
    adapter_output = adapter_scale * jnp.einsum(
        "srk,kd->srd", rank_projected, local_b, precision=lax.Precision.HIGHEST
    )
    return (base_sum + adapter_output).astype(jnp.bfloat16)


def solution(mesh):
    return jax.shard_map(
        body,
        mesh=mesh,
        in_specs=(
            P(None, "group", "tensor"),
            P(None, "group", "tensor"),
            P(None, "group", "tensor"),
            P("group", None, "tensor"),
            P("group", None, "tensor"),
            P("group"),
            P("tensor", None),
            P("group", None),
            P(None, "group"),
        ),
        out_specs=P(None, "group", "tensor"),
        check_vma=False,
    )
```

profile of v0, /device:TPU:2, one launch (start us, length us, event | category | flops | bytes accessed | tf_op | source)
XLA Modules:
  0.0 263.8 jit_solution(11034344880601579959)
XLA Ops:
  6.5 1.6 convert_element_type.124
  8.2 1.4 slice_bitcast_fusion.4
  9.6 1.0 copy.30
  10.6 1.4 bitcast_convert_fusion
  12.0 1.6 copy.31
  13.6 2.0 slice_bitcast_fusion
  16.5 1.6 fusion.58
  18.1 1.7 fusion.60
  19.7 2.0 fusion.57
  21.7 2.0 fusion.59
  23.7 2.1 fusion.56
  25.8 1.5 copy.25
  27.3 1.7 fusion.47
  30.6 1.4 fusion.15
  33.0 2.2 fusion.11
  35.3 1.1 convert_element_type.109
  37.6 1.1 fusion.39
  38.7 1.3 fusion.40
  40.0 1.2 fusion.12
  41.2 1.1 convert_element_type.113
  43.5 1.2 fusion.27
  44.7 1.3 fusion.29
  46.6 1.0 copy.41
  47.6 1.3 fusion.62
  50.3 1.3 fusion.30
  52.3 22.2 %all-gather.2.cloned.1.call-done = bf16[8192,64]{0,1:T(8,128)(2,1)} async-done(((bf16[256,64]{0,1:T(8,128)(2,1)}), bf16[8192,64]{0,1:T(8,128)(2,1)}) %all-gather.2.cloned.1.call-update) | async-done | bytes 1048592 | tf_op jit(solution)/shard_map/all_gather | solution.py:73
  74.4 2.0 convolution_convert_fusion
  76.7 9.4 %fusion.2 = bf16[4,128,4096]{2,1,0:T(8,128)(2,1)} fusion(bf16[4,128,1024]{2,1,0:T(8,128)(2,1)S(1)} %constant_dynamic-update-slice_fusion, bf16[1024,4096]{1,0:T(8,128)(2,1)} %param.15), kind=kOutput, calls=%fused_computation.2 | convolution fusion | flops 4297064448 | bytes 13631488 | tf_op jit(solution)/shard_map/srw,wd->srd/dot_general | solution.py:95
  86.1 32.4 %all_gather.7 = bf16[64,4096]{1,0:T(8,128)(2,1)S(1)} all-gather(bf16[64,128]{1,0:T(8,128)(2,1)S(1)} %convert_element_type.126), channel_id=1, replica_groups=mesh['group'=32,'tensor'=8] {'group'}, dimensions={1}, use_global_device_ids=true | all-gather | bytes 540672 | tf_op jit(solution)/shard_map/all_gather | solution.py:76
  118.6 44.4 %all-reduce.2.cloned.1.call-done = bf16[4,128,64]{1,2,0:T(8,128)(2,1)} async-done(((bf16[4,128,64]{1,2,0:T(8,128)(2,1)}), bf16[4,128,64]{1,2,0:T(8,128)(2,1)}) %all-reduce.2.cloned.1.call-update) | async-done | bytes 65552 | tf_op jit(solution)/shard_map/psum | solution.py:108
  162.9 92.1 %reduce-scatter.2.cloned.1.call-done = bf16[4,128,512]{2,1,0:T(8,128)(2,1)} async-done(((bf16[4,128,4096]{2,1,0:T(8,128)(2,1)}), bf16[4,128,512]{2,1,0:T(8,128)(2,1)}) %reduce-scatter.2.cloned.1.call-update) | async-done | bytes 524304 | tf_op jit(solution)/shard_map/reduce_scatter | solution.py:98
  255.1 2.2 fusion.6
  (43 shorter events, 8.9 us)
Async XLA Ops:
  6.5 26.5 %copy-start = (bf16[128,32,128]{2,1,0:T(8,128)(2,1)S(1)}, bf16[128,32,128]{2,1,0:T(8,128)(2,1)}, u32[]{:S(2)}) copy-start(bf16[128,32,128]{2,1,0:T(8,128)(2,1)} %param.13) | copy-start | bytes 3145732
  6.5 17.2 %copy-start.1 = (bf16[128,32,128]{2,1,0:T(8,128)(2,1)S(1)}, bf16[128,32,128]{2,1,0:T(8,128)(2,1)}, u32[]{:S(2)}) copy-start(bf16[128,32,128]{2,1,0:T(8,128)(2,1)} %param.12) | copy-start | bytes 3145732
  6.5 67.9 %all-gather.2.cloned.1.call-start = ((), (), s32[]{:S(2)}) async-start(), calls=%async_computation.2 | async-start | bytes 1081344 | tf_op jit(solution)/shard_map/all_gather | solution.py:73
  8.2 154.8 %all-reduce.2.cloned.1.call-start = ((), (), s32[]{:S(2)}) async-start(), calls=%async_computation.3 | async-start | bytes 131072 | tf_op jit(solution)/shard_map/psum | solution.py:108
  76.4 9.7 %copy-start.2 = (f32[64,128]{1,0:T(8,128)S(1)}, f32[64,128]{1,0:T(8,128)}, u32[]{:S(2)}) copy-start(f32[64,128]{1,0:T(8,128)} %param.17) | copy-start | bytes 98308
  76.4 178.6 %reduce-scatter.2.cloned.1.call-start = ((), (), s32[]{:S(2)}) async-start(), calls=%async_computation.1 | async-start | bytes 4718592 | tf_op jit(solution)/shard_map/reduce_scatter | solution.py:98
Sparse Core Ops, SparseCore 0:
  9.1 65.2 all-gather.1
  77.0 85.8 all-reduce.1
  167.6 87.4 reduce-scatter.1
where the time goes:
time: 266 us; the launch traced here: 264 us
  waiting for transfers between devices  159 us (60%)
  matrix products  34.7 us (13%)
  blocking collectives  32.4 us (12%)
  between operations  13.4 us (5%)
  local copies, waits for them, and re-layouts  12.3 us (5%)
  other arithmetic  11.9 us (4%)
    reduce_scatter x1, waiting for transfers between devices, body(): lax.psum_scatter(partial_term.astype(jnp.bfloat16), 'tensor', scatter_dim...  92.1 us
    psum x1, waiting for transfers between devices, body(): lax.psum(local_proj.astype(jnp.bfloat16), 'tensor').astype(jnp.float32)  44.4 us
    all_gather x1, blocking collectives, body(): lax.all_gather(up_factor.astype(jnp.bfloat16), 'group', axis=1, tiled=True)  32.4 us
    all_gather x1, waiting for transfers between devices, body(): lax.all_gather(down_factor.astype(jnp.bfloat16), 'group', axis=0, tiled=T...  22.2 us
    dot_general x1, matrix products, body(): jnp.einsum('srw,wd->srd', attention_context, output_weight, preferred_ele...  9.42 us
    dot_general x4, matrix products, attend(): jnp.einsum('rkgd,rckd->rkgc', query_h, keys_c, preferred_element_type=jnp...  6.71 us
    dot_general x4, matrix products, attend(): jnp.einsum('rkgd,trkd->rkgt', query_h, keys_n, preferred_element_type=jnp...  6.18 us
    unnamed x16, local copies, waits for them, and re-layouts  5.86 us
  transfers between devices with their start and end apart: 3, of which 3 were waited for; matrix products, arithmetic and copies ran while one was open for 20% of the time, Pallas kernels for 0%

commit v1 on v0

v1 whole, which is shorter than its diff:
```python
import functools
import math

import jax
import jax.numpy as jnp
from jax import lax
from jax.experimental import pallas as pl
from jax.experimental.pallas import tpu as pltpu
from jax.sharding import PartitionSpec as P

MESH = pl.DeviceIdType.MESH
BF = jnp.bfloat16
F32 = jnp.float32

STEPS = 4
ROWS = 128
HEADS = 8
D = 128
CACHE = 32
WIDTH = HEADS * D
COLS = 512
HALF = COLS // 2
CHUNK = 32
CHUNKS = ROWS // CHUNK
M = STEPS * CHUNK
ADAPTER_SCALE = 2.0
NEG = -1e30
EXP2_SCALE = math.log2(math.e) / math.sqrt(D)

TREE2 = {
    (1, 1): (0, 1),
    (2, 1): (3, 1),
    (0, 1): (0, 0),
    (3, 1): (3, 0),
    (2, 0): (1, 0),
    (1, 0): (0, 0),
    (3, 0): (0, 0),
}


def mirror(tree):
    flip = lambda n: ((4 - n[0]) % 4, n[1])
    return {flip(a): flip(b) for a, b in tree.items()}


def children(tree, node):
    return [a for a, b in tree.items() if b == node]


def level(tree, node):
    kids = children(tree, node)
    return 0 if not kids else 1 + max(level(tree, k) for k in kids)


def trees_of(chunk):
    return (TREE2, mirror(TREE2))


NODES = [(r, o) for r in (2, 1, 3, 0) for o in (1, 0)]
EDGES = [n for n in NODES if n != (0, 0)]


def block_order():
    trees = trees_of(0)
    items = [(level(trees[h], n), i, h, n) for i, n in enumerate(NODES) for h in (0, 1)]
    items.sort(key=lambda t: (t[0], t[1], t[2]))
    return [(n, h) for _, _, h, n in items]


BLOCKS = block_order()
BLOCK_INDEX = {b: i for i, b in enumerate(BLOCKS)}
EDGE_INDEX = {(n, h): 2 * i + h for i, n in enumerate(EDGES) for h in (0, 1)}


def kernel(
    q_ref, ks_ref, vs_ref, kc_ref, vc_ref, len_ref, w_ref, d_ref, u_ref, o_ref,
    q_v, ks_v, vs_v, kc_v, vc_v, w_v, d_v, u_v, ctx_v, part_v, recv_v, fac_v, proj_v, prcv_v, out_v,
    in_sem, w_sem, send_sem, recv_sem, zsend_sem, zrecv_sem, qsend_sem, qrecv_sem, psend_sem, precv_sem, out_sem,
):
    g = lax.axis_index("group")
    t = lax.axis_index("tensor")
    z, quad = g // 4, g % 4
    y, xh = t // 2, t % 2
    dev = lambda gg, yy, xx: (gg, yy * 2 + xx)
    y_up = dev(g, (y + 1) % 4, xh)
    y_down = dev(g, (y + 3) % 4, xh)
    x_peer = dev(g, y, 1 - xh)
    z_peers = [(((z + k) % 8) * 4 + quad, t) for k in range(1, 8)]
    quad_ids = [(quad + k) % 4 for k in range(1, 4)]
    quad_peers = [(z * 4 + k, t) for k in quad_ids]

    barrier = pltpu.get_barrier_semaphore()
    peers = [y_up, y_down, x_peer] + z_peers + quad_peers
    for p in peers:
        pl.semaphore_signal(barrier, inc=1, device_id=p, device_id_type=MESH)

    def fetch(src, dst, sem):
        c = pltpu.make_async_copy(src, dst, sem)
        c.start()
        return c

    first = pl.ds(0, CHUNK)
    rest = pl.ds(CHUNK, ROWS - CHUNK)
    loads = []
    for k, rows in enumerate((first, rest)):
        loads.append([
            fetch(q_ref.at[:, rows, :], q_v.at[:, rows, :], in_sem.at[k, 0]),
            fetch(kc_ref.at[rows], kc_v.at[rows], in_sem.at[k, 1]),
            fetch(vc_ref.at[rows], vc_v.at[rows], in_sem.at[k, 2]),
        ])
        if k == 0:
            loads[0] += [
                fetch(ks_ref, ks_v, in_sem.at[k, 3]),
                fetch(vs_ref, vs_v, in_sem.at[k, 4]),
            ]
            fac_loads = [
                fetch(d_ref, d_v, in_sem.at[1, 3]),
                fetch(u_ref, u_v, in_sem.at[1, 4]),
            ]

            w_loads = []

            def load_w(i):
                (r, o), h = BLOCKS[i]
                dest = ((y + 4 - r) % 4) * 2 + ((xh + o) % 2)
                cols = pl.ds(pl.multiple_of(dest * COLS + h * HALF, HALF), HALF)
                w_loads.append(fetch(w_ref.at[:, cols], w_v.at[i], w_sem.at[i]))

            for i in range(6):
                load_w(i)
    for i in range(6, len(BLOCKS)):
        load_w(i)

    def attention(chunk):
        row0 = chunk * CHUNK
        ks_c = ks_v[:, row0:row0 + CHUNK, :].reshape(STEPS * CHUNK, D)
        vs_c = vs_v[:, row0:row0 + CHUNK, :].reshape(STEPS * CHUNK, D)
        ones = jnp.ones((STEPS * CHUNK, D), BF)
        vs_ext = jnp.concatenate([vs_c, ones], axis=1)
        sub = lax.broadcasted_iota(jnp.int32, (8, 2 * D), 0)
        lane = lax.broadcasted_iota(jnp.int32, (8, 2 * D), 1)

        def sixteen(jj, carry):
            r0 = pl.multiple_of(row0 + jj * 16, 16)
            qf = q_v[:, pl.ds(r0, 16), :].astype(F32)
            outs = []
            for part in range(2):
                qb = jnp.concatenate(
                    [
                        qf[s, part * 8:part * 8 + 8, h * D:(h + 1) * D]
                        for s in range(STEPS)
                        for h in range(HEADS)
                    ],
                    axis=0,
                ).astype(BF)
                rp = r0 + part * 8
                k8 = kc_v[pl.ds(rp, 8)].reshape(8 * CACHE, D)
                v8 = vc_v[pl.ds(rp, 8)].reshape(8 * CACHE, D)
                contract = (((1,), (1,)), ((), ()))
                s1 = lax.dot_general(qb, k8, contract, preferred_element_type=F32)
                s2 = lax.dot_general(qb, ks_c, contract, preferred_element_type=F32)
                lens = jnp.zeros((8, 2 * D), jnp.int32)
                for i in range(8):
                    lens = jnp.where(sub == i, len_ref[rp + i], lens)
                ok1 = (lane // CACHE == sub) & (lane % CACHE < lens)
                bias1 = jnp.where(ok1, 0.0, NEG).astype(F32)
                sub2, lane2 = sub[:, :D], lane[:, :D]
                mine = lane2 % CHUNK == sub2 + (jj * 16 + part * 8)
                bias2 = jnp.stack(
                    [
                        jnp.where(mine & (lane2 // CHUNK <= s), 0.0, NEG).astype(F32)
                        for s in range(STEPS)
                    ]
                )
                s1 = s1.reshape(STEPS * HEADS, 8, 2 * D) + bias1[None]
                s2 = s2.reshape(STEPS, HEADS, 8, D) + bias2[:, None]
                s1 = s1.reshape(STEPS * HEADS * 8, 2 * D)
                s2 = s2.reshape(STEPS * HEADS * 8, D)
                top = jnp.maximum(jnp.maximum(s1[:, :D], s1[:, D:]), s2)
                top = jnp.max(top, axis=1, keepdims=True)
                p1 = jnp.exp2((s1 - top) * EXP2_SCALE).astype(BF)
                p2 = jnp.exp2((s2 - top) * EXP2_SCALE).astype(BF)
                v_ext = jnp.concatenate([v8, jnp.ones((8 * CACHE, D), BF)], axis=1)
                acc = jnp.dot(p1, v_ext, preferred_element_type=F32) + jnp.dot(
                    p2, vs_ext, preferred_element_type=F32
                )
                outs.append(acc[:, :D] / acc[:, D:])
            for s in range(STEPS):
                for h in range(HEADS):
                    i = (s * HEADS + h) * 8
                    tile = jnp.concatenate([outs[0][i:i + 8], outs[1][i:i + 8]], axis=0)
                    ctx_v[chunk, pl.ds(pl.multiple_of(s * CHUNK + jj * 16, 16), 16), h * D:(h + 1) * D] = (
                        tile.astype(BF)
                    )
            return carry

        lax.fori_loop(0, CHUNK // 16, sixteen, 0)

    def product(chunk, b):
        i = BLOCK_INDEX[b]
        if chunk == 0:
            w_loads[i].wait()
        part_v[chunk, i] = jnp.dot(ctx_v[chunk], w_v[i], preferred_element_type=F32).astype(BF)

    sends = []

    def target_of(node, parent):
        if node[1] != parent[1]:
            return x_peer
        return y_up if (parent[0] - node[0]) % 4 == 1 else y_down

    def edge_copy(chunk, node, h):
        e = EDGE_INDEX[(node, h)]
        parent = trees_of(chunk)[h][node]
        return pltpu.make_async_remote_copy(
            src_ref=part_v.at[chunk, BLOCK_INDEX[(node, h)]],
            dst_ref=recv_v.at[chunk, e],
            send_sem=send_sem.at[chunk, e],
            recv_sem=recv_sem.at[chunk, e],
            device_id=target_of(node, parent),
            device_id_type=MESH,
        )

    def send(chunk, node, h):
        c = edge_copy(chunk, node, h)
        c.start()
        sends.append(c)

    def combine(chunk, node, h):
        i = BLOCK_INDEX[(node, h)]
        total = part_v[chunk, i].astype(F32)
        for kid in children(trees_of(chunk)[h], node):
            edge_copy(chunk, kid, h).wait_recv()
            total = total + recv_v[chunk, EDGE_INDEX[(kid, h)]].astype(F32)
        part_v[chunk, i] = total.astype(BF)
        send(chunk, node, h)

    def at_level(chunk, lv):
        trees = trees_of(chunk)
        return [(n, h) for n, h in BLOCKS if n != (0, 0) and level(trees[h], n) == lv]

    owner = z == t
    z_copies = [
        pltpu.make_async_remote_copy(
            src_ref=fac_v.at[quad], dst_ref=fac_v.at[quad],
            send_sem=zsend_sem.at[k], recv_sem=zrecv_sem.at[0],
            device_id=z_peers[k], device_id_type=MESH,
        )
        for k in range(7)
    ]
    quad_copies = [
        pltpu.make_async_remote_copy(
            src_ref=fac_v.at[quad], dst_ref=fac_v.at[quad],
            send_sem=qsend_sem.at[k], recv_sem=qrecv_sem.at[2 - k],
            device_id=quad_peers[k], device_id_type=MESH,
        )
        for k in range(3)
    ]

    def factors_out():
        for c in fac_loads:
            c.wait()

        @pl.when(owner)
        def _():
            fac_v[quad, 0:D, :] = jnp.concatenate([d_v[0:D, :], d_v[D:2 * D, :]], axis=1).astype(BF)
            fac_v[quad, D:D + 64, :] = u_v[...].astype(BF)
            for c in z_copies:
                c.start()

    def factors_quad():
        @pl.when(jnp.logical_not(owner))
        def _():
            z_copies[0].wait_recv()

        for c in quad_copies:
            c.start()

    def factors_wait():
        for c in quad_copies:
            c.wait_recv()

    lane_m = lax.broadcasted_iota(jnp.int32, (2 * M, D), 1)

    def project():
        halves = []
        for k in range(2):
            lo = jnp.zeros((2 * M, D), F32)
            hi = jnp.zeros((2 * M, D), F32)
            ctx = ctx_v[2 * k:2 * k + 2].reshape(2 * M, WIDTH)
            for j in range(4):
                f = fac_v[j, 0:D, :]
                lo = lo + jnp.dot(ctx[:, 2 * j * D:(2 * j + 1) * D], f, preferred_element_type=F32)
                hi = hi + jnp.dot(ctx[:, (2 * j + 1) * D:(2 * j + 2) * D], f, preferred_element_type=F32)
            if k == 0:
                halves.append(lo + pltpu.roll(hi, 64, 1))
            else:
                halves.append(hi + pltpu.roll(lo, 64, 1))
        proj_v[0] = jnp.where(lane_m < 64, halves[0], halves[1]).astype(BF)

    y_pair = dev(g, y + 1 - 2 * (y % 2), xh)
    y_flip = dev(g, 3 - y, xh)
    p_copies = [
        pltpu.make_async_remote_copy(
            src_ref=proj_v.at[k], dst_ref=prcv_v.at[k],
            send_sem=psend_sem.at[k], recv_sem=precv_sem.at[k],
            device_id=p, device_id_type=MESH,
        )
        for k, p in enumerate((x_peer, y_pair, y_flip))
    ]

    def proj_step(k):
        p_copies[k].wait_recv()
        proj_v[k + 1] = (proj_v[k].astype(F32) + prcv_v[k].astype(F32)).astype(BF)
        if k < 2:
            p_copies[k + 1].start()

    outs = []

    def finish(chunk):
        proj = proj_v[3, pl.ds((chunk % 2) * M, M), :]
        lane = lax.broadcasted_iota(jnp.int32, (M, D), 1)
        keep = lane < 64 if chunk < 2 else lane >= 64
        proj = jnp.where(keep, proj.astype(F32) * ADAPTER_SCALE, 0.0).astype(BF)
        for h in range(2):
            total = part_v[chunk, BLOCK_INDEX[((0, 0), h)]].astype(F32)
            for kid in children(trees_of(chunk)[h], (0, 0)):
                edge_copy(chunk, kid, h).wait_recv()
                total = total + recv_v[chunk, EDGE_INDEX[(kid, h)]].astype(F32)
            for j in range(2):
                u = fac_v[2 * h + j, D:D + 64, :]
                low = jnp.dot(proj, jnp.concatenate([u, u], axis=0), preferred_element_type=F32)
                res = (total[:, j * D:(j + 1) * D] + low).astype(BF)
                out_v[:, chunk * CHUNK:(chunk + 1) * CHUNK, h * HALF + j * D:h * HALF + (j + 1) * D] = (
                    res.reshape(STEPS, CHUNK, D)
                )
        rows = pl.ds(chunk * CHUNK, CHUNK)
        outs.append(fetch(out_v.at[:, rows, :], o_ref.at[:, rows, :], out_sem.at[chunk]))

    for chunk in range(CHUNKS):
        if chunk < 2:
            for c in loads[chunk]:
                c.wait()
        attention(chunk)
        if chunk == 0:
            pl.semaphore_wait(barrier, len(peers))
            factors_out()
        trees = trees_of(chunk)
        for n, h in BLOCKS:
            product(chunk, (n, h))
            if level(trees[h], n) == 0:
                send(chunk, n, h)
        if chunk == 1:
            factors_quad()
        if chunk >= 1:
            for n, h in at_level(chunk - 1, 1):
                combine(chunk - 1, n, h)
    factors_wait()
    project()
    p_copies[0].start()
    last = CHUNKS - 1
    for n, h in at_level(last, 1):
        combine(last, n, h)
    for chunk in range(CHUNKS):
        for n, h in at_level(chunk, 2):
            combine(chunk, n, h)
        if chunk < 3:
            proj_step(chunk)
    for chunk in range(CHUNKS):
        finish(chunk)

    for c in sends:
        c.wait_send()

    @pl.when(owner)
    def _():
        for c in z_copies:
            c.wait_send()

    for c in quad_copies + p_copies:
        c.wait_send()
    for c in outs:
        c.wait()


def body(q, ks, vs, kc, vc, lengths, w, d, u):
    any_spec = pl.BlockSpec(memory_space=pl.ANY)
    smem = pl.BlockSpec(memory_space=pltpu.SMEM)
    dma = pltpu.SemaphoreType.DMA
    return pl.pallas_call(
        kernel,
        out_shape=jax.ShapeDtypeStruct((STEPS, ROWS, COLS), BF),
        in_specs=[any_spec] * 5 + [smem] + [any_spec] * 3,
        out_specs=any_spec,
        scratch_shapes=[
            pltpu.VMEM((STEPS, ROWS, WIDTH), BF),
            pltpu.VMEM((STEPS, ROWS, D), BF),
            pltpu.VMEM((STEPS, ROWS, D), BF),
            pltpu.VMEM((ROWS, CACHE, D), BF),
            pltpu.VMEM((ROWS, CACHE, D), BF),
            pltpu.VMEM((16, WIDTH, HALF), BF),
            pltpu.VMEM((256, 64), F32),
            pltpu.VMEM((64, 128), F32),
            pltpu.VMEM((CHUNKS, M, WIDTH), BF),
            pltpu.VMEM((CHUNKS, 16, M, HALF), BF),
            pltpu.VMEM((CHUNKS, 14, M, HALF), BF),
            pltpu.VMEM((4, D + 64, D), BF),
            pltpu.VMEM((4, 2 * M, D), BF),
            pltpu.VMEM((3, 2 * M, D), BF),
            pltpu.VMEM((STEPS, ROWS, COLS), BF),
            dma((2, 5)),
            dma((16,)),
            dma((CHUNKS, 14)),
            dma((CHUNKS, 14)),
            dma((7,)),
            dma((1,)),
            dma((3,)),
            dma((3,)),
            dma((3,)),
            dma((3,)),
            dma((CHUNKS,)),
        ],
        compiler_params=pltpu.CompilerParams(
            collective_id=1, has_side_effects=True, vmem_limit_bytes=48 << 20
        ),
        cost_estimate=pl.CostEstimate(
            flops=2 * 512 * 1024 * 4200, bytes_accessed=13 << 20, transcendentals=1 << 20
        ),
        name="attend_project_reduce",
    )(q, ks, vs, kc, vc, lengths, w, d, u)


def solution(mesh):
    return jax.shard_map(
        body,
        mesh=mesh,
        in_specs=(
            P(None, "group", "tensor"),
            P(None, "group", "tensor"),
            P(None, "group", "tensor"),
            P("group", None, "tensor"),
            P("group", None, "tensor"),
            P("group"),
            P("tensor", None),
            P("group", None),
            P(None, "group"),
        ),
        out_specs=P(None, "group", "tensor"),
        check_vma=False,
    )
```

time: 266 us -> 63.7 us (0.24)
  waiting for transfers between devices: 159 us -> 0 us
  Pallas kernels: 0 us -> 53.8 us
  matrix products: 34.7 us -> 0 us
  blocking collectives: 32.4 us -> 0 us
  between operations: 13.4 us -> 0.03 us
  other arithmetic: 11.9 us -> 0 us
  local copies, waits for them, and re-layouts: 12.3 us -> 8.62 us
    reduce_scatter x1 -> x0, waiting for transfers between devices: 92.1 us -> none  [body(): lax.psum_scatter(partial_term.astype(jnp.bfloat16), 'tensor', scatter_dim...]
    pallas_call x0 -> x1, Pallas kernels: none -> 53.8 us  [body(): pl.pallas_call(kernel, out_shape=jax.ShapeDtypeStruct((STEPS, ROWS, COLS)...]
    psum x1 -> x0, waiting for transfers between devices: 44.4 us -> none  [body(): lax.psum(local_proj.astype(jnp.bfloat16), 'tensor').astype(jnp.float32)]
    dot_general x18 -> x0, matrix products: 34.7 us -> none  [the longest x1 9.42 us: body(): jnp.einsum('srw,wd->srd', attention_context, output_weight, preferred_ele...]
    all_gather x1 -> x0, blocking collectives: 32.4 us -> none  [body(): lax.all_gather(up_factor.astype(jnp.bfloat16), 'group', axis=1, tiled=True)]
    all_gather x1 -> x0, waiting for transfers between devices: 22.2 us -> none  [body(): lax.all_gather(down_factor.astype(jnp.bfloat16), 'group', axis=0, tiled=T...]
    reduce_sum x7 -> x0, other arithmetic: 5.06 us -> none  [the longest x3 2.54 us: attend(): jnp.sum(fresh_exp, axis=-1, keepdims=True)]
    unnamed x16, local copies, waits for them, and re-layouts: 5.86 us -> 8.62 us
  transfers between devices with their start and end apart: 3 -> 0, of which waited for: 3 -> 0; matrix products, arithmetic and copies ran while one was open for 20% -> 0% of each run, Pallas kernels for 0% -> 0%
where the time goes in v1:
time: 63.7 us; the launch traced here: 62.5 us
  Pallas kernels  53.8 us (84%)
  local copies, waits for them, and re-layouts  8.62 us (14%)
    pallas_call x1, Pallas kernels, body(): pl.pallas_call(kernel, out_shape=jax.ShapeDtypeStruct((STEPS, ROWS, COLS)...  53.8 us
    unnamed x16, local copies, waits for them, and re-layouts  8.62 us

profile of v1, /device:TPU:2, one launch (start us, length us, event | category | flops | bytes accessed | tf_op | source)
XLA Modules:
  0.0 62.5 jit_solution(16346791423451137378)
XLA Ops:
  0.0 0.9 %copy.10.d_ref = f32[256,64]{1,0:T(8,128)S(1)} copy(f32[256,64]{0,1:T(8,128)} %param.16) | data formatting | bytes 131072 | tf_op args[7]
  0.9 0.0 copy-start
  0.9 1.2 %copy-done = bf16[4,128,1024]{2,1,0:T(8,128)(2,1)S(1)} copy-done((bf16[4,128,1024]{2,1,0:T(8,128)(2,1)S(1)}, bf16[4,128,1024]{2,1,0:T(8,128)(2,1)}, u32[]{:S(2)}) %copy-start) | copy-done | bytes 1048600
  2.2 0.0 copy-start.1
  2.2 1.2 %copy-done.1 = bf16[128,32,128]{2,1,0:T(8,128)(2,1)S(1)} copy-done((bf16[128,32,128]{2,1,0:T(8,128)(2,1)S(1)}, bf16[128,32,128]{2,1,0:T(8,128)(2,1)}, u32[]{:S(2)}) %copy-start.1) | copy-done | bytes 1048600
  3.4 0.0 copy-start.2
  3.4 1.2 %copy-done.2 = bf16[128,32,128]{2,1,0:T(8,128)(2,1)S(1)} copy-done((bf16[128,32,128]{2,1,0:T(8,128)(2,1)S(1)}, bf16[128,32,128]{2,1,0:T(8,128)(2,1)}, u32[]{:S(2)}) %copy-start.2) | copy-done | bytes 1048600
  4.6 0.0 copy-start.3
  4.6 0.9 %copy-done.3 = bf16[4,128,128]{2,1,0:T(8,128)(2,1)S(1)} copy-done((bf16[4,128,128]{2,1,0:T(8,128)(2,1)S(1)}, bf16[4,128,128]{2,1,0:T(8,128)(2,1)}, u32[]{:S(2)}) %copy-start.3) | copy-done | bytes 131096
  5.5 0.0 copy-start.4
  5.5 0.9 %copy-done.4 = bf16[4,128,128]{2,1,0:T(8,128)(2,1)S(1)} copy-done((bf16[4,128,128]{2,1,0:T(8,128)(2,1)S(1)}, bf16[4,128,128]{2,1,0:T(8,128)(2,1)}, u32[]{:S(2)}) %copy-start.4) | copy-done | bytes 131096
  6.4 0.0 copy-start.5
  6.4 0.8 %copy-done.5 = f32[64,128]{1,0:T(8,128)S(1)} copy-done((f32[64,128]{1,0:T(8,128)S(1)}, f32[64,128]{1,0:T(8,128)}, u32[]{:S(2)}) %copy-start.5) | copy-done | bytes 32792
  7.2 0.0 copy-start.6
  7.2 0.7 %copy-done.6 = s32[128]{0:T(128)S(1)} copy-done((s32[128]{0:T(128)S(1)}, s32[128]{0:T(128)}, u32[]{:S(2)}) %copy-start.6) | copy-done | bytes 536
  7.8 53.8 %attend_project_reduce.1 = bf16[4,128,512]{2,1,0:T(8,128)(2,1)S(1)} custom-call(bf16[4,128,1024]{2,1,0:T(8,128)(2,1)S(1)} %copy-done, bf16[4,128,128]{2,1,0:T(8,128)(2,1)S(1)} %copy-done.3, bf16[4,128,128]{2,1,0:T(8,128)(2,1)S(1)} %copy-done.4, bf16[128,32,128]{2,1,0:T(8,128)(2,1)S(1)} %copy-done.1, bf16[128,32,128]{2,1,0:T(8,128)(2,1)S(1)} %copy-done.2, ...), custom_call_target="tpu_custom_call" | custom-call | flops 4404019200 | bytes 13631488 | tf_op jit(solution)/shard_map/attend_project_reduce/pallas_call | solution.py:390
  61.7 0.8 %copy.12 = bf16[4,128,512]{2,1,0:T(8,128)(2,1)} copy(bf16[4,128,512]{2,1,0:T(8,128)(2,1)S(1)} %attend_project_reduce.1) | data formatting | bytes 1048576
Async XLA Ops:
  0.9 1.2 %copy-start = (bf16[4,128,1024]{2,1,0:T(8,128)(2,1)S(1)}, bf16[4,128,1024]{2,1,0:T(8,128)(2,1)}, u32[]{:S(2)}) copy-start(bf16[4,128,1024]{2,1,0:T(8,128)(2,1)} %q_ref.1) | copy-start | bytes 3145732
  2.2 1.2 %copy-start.1 = (bf16[128,32,128]{2,1,0:T(8,128)(2,1)S(1)}, bf16[128,32,128]{2,1,0:T(8,128)(2,1)}, u32[]{:S(2)}) copy-start(bf16[128,32,128]{2,1,0:T(8,128)(2,1)} %kc_ref.1) | copy-start | bytes 3145732
  3.4 1.2 %copy-start.2 = (bf16[128,32,128]{2,1,0:T(8,128)(2,1)S(1)}, bf16[128,32,128]{2,1,0:T(8,128)(2,1)}, u32[]{:S(2)}) copy-start(bf16[128,32,128]{2,1,0:T(8,128)(2,1)} %vc_ref.1) | copy-start | bytes 3145732
  4.6 0.9 %copy-start.3 = (bf16[4,128,128]{2,1,0:T(8,128)(2,1)S(1)}, bf16[4,128,128]{2,1,0:T(8,128)(2,1)}, u32[]{:S(2)}) copy-start(bf16[4,128,128]{2,1,0:T(8,128)(2,1)} %ks_ref.1) | copy-start | bytes 393220
  5.5 0.9 %copy-start.4 = (bf16[4,128,128]{2,1,0:T(8,128)(2,1)S(1)}, bf16[4,128,128]{2,1,0:T(8,128)(2,1)}, u32[]{:S(2)}) copy-start(bf16[4,128,128]{2,1,0:T(8,128)(2,1)} %vs_ref.1) | copy-start | bytes 393220
  6.4 0.8 %copy-start.5 = (f32[64,128]{1,0:T(8,128)S(1)}, f32[64,128]{1,0:T(8,128)}, u32[]{:S(2)}) copy-start(f32[64,128]{1,0:T(8,128)} %u_ref.1) | copy-start | bytes 98308
  7.2 0.7 %copy-start.6 = (s32[128]{0:T(128)S(1)}, s32[128]{0:T(128)}, u32[]{:S(2)}) copy-start(s32[128]{0:T(128)} %len_ref.1) | copy-start | bytes 1540

commit v2 on v1

v2 whole, which is shorter than its diff:
```python
import functools
import math

import jax
import jax.numpy as jnp
from jax import lax
from jax.experimental import pallas as pl
from jax.experimental.pallas import tpu as pltpu
from jax.sharding import PartitionSpec as P

MESH = pl.DeviceIdType.MESH
BF = jnp.bfloat16
F32 = jnp.float32

STEPS = 4
ROWS = 128
HEADS = 8
D = 128
CACHE = 32
WIDTH = HEADS * D
COLS = 512
HALF = COLS // 2
GROUP = 32
CHUNK_ROWS = (32, 32, 32, 32)
CHUNK_TREES = (3, 1, 3, 2)
ROW0 = [sum(CHUNK_ROWS[:c]) for c in range(len(CHUNK_ROWS))]
CHUNKS = len(CHUNK_ROWS)
ADAPTER_SCALE = 2.0
NEG = -1e30
EXP2_SCALE = math.log2(math.e) / math.sqrt(D)

TREES = {
    1: {(2, 1): (1, 1), (1, 1): (0, 1), (3, 1): (0, 1), (0, 1): (0, 0), (2, 0): (1, 0), (1, 0): (0, 0), (3, 0): (0, 0)},
    2: {(1, 1): (0, 1), (2, 1): (3, 1), (0, 1): (0, 0), (3, 1): (3, 0), (2, 0): (1, 0), (1, 0): (0, 0), (3, 0): (0, 0)},
    3: {(1, 1): (0, 1), (2, 1): (2, 0), (3, 1): (3, 0), (0, 1): (0, 0), (2, 0): (1, 0), (1, 0): (0, 0), (3, 0): (0, 0)},
    4: {(1, 1): (1, 0), (2, 1): (2, 0), (3, 1): (3, 0), (0, 1): (0, 0), (2, 0): (1, 0), (1, 0): (0, 0), (3, 0): (0, 0)},
}


def mirror(tree):
    flip = lambda n: ((4 - n[0]) % 4, n[1])
    return {flip(a): flip(b) for a, b in tree.items()}


def trees_of(chunk):
    tree = TREES[CHUNK_TREES[chunk]]
    return (tree, mirror(tree))


def children(tree, node):
    return [a for a, b in tree.items() if b == node]


NODES = [(r, o) for r in (2, 1, 3, 0) for o in (1, 0)]
ROOT = (0, 0)
EDGE_INDEX = {(n, h): 2 * i + h for i, n in enumerate(NODES[:-1]) for h in (0, 1)}

ORDER = (
    "A0", "O", "L0210", "L0211", "L0110", "L0310", "L0111", "L0311", "A1", "L1210", "L1211", "L1200", "L1310",
    "L1201", "L1111", "L1300", "C0200", "C0010", "L1101", "C0011", "A2", "C0201", "C0300", "C1110", "C1311",
    "L2210", "C1100", "Q", "L2211", "L2110", "C0101", "L2310", "L2111", "L2311", "M0100", "M0301", "C1301",
    "M0000", "M0001", "M1010", "M1011", "M1000", "M1001", "M2200", "M2201", "C0100", "M2100", "M2300", "M2010",
    "M2101", "M2301", "M2011", "M2000", "M2001", "A3", "C0301", "C1010", "C2200", "L3210", "L3211", "L3200",
    "L3110", "L3201", "L3311", "M3310", "P", "C1011", "M3111", "M3100", "M3300", "M3010", "M3101", "M3301",
    "C2201", "C2010", "C2011", "M3011", "M3000", "M3001", "C2300", "C2101", "C2100", "C3310", "R", "C3111",
    "C3301", "C3100", "C3011", "C3010", "C2301", "C3300", "R", "C3101", "R", "F0", "F1", "F2", "F3",
)
STEPS_IN_ORDER = [(w[0], tuple(int(x) for x in w[1:])) for w in ORDER]


def block_order():
    seen = []
    for kind, v in STEPS_IN_ORDER:
        if kind in "LMC":
            b = ((v[1], v[2]), v[3])
            if b not in seen:
                seen.append(b)
        elif kind == "F":
            for b in ((ROOT, 0), (ROOT, 1)):
                if b not in seen:
                    seen.append(b)
    return seen


BLOCKS = block_order()
BLOCK_INDEX = {b: i for i, b in enumerate(BLOCKS)}


def kernel(
    q_ref, ks_ref, vs_ref, kc_ref, vc_ref, len_ref, w_ref, d_ref, u_ref, o_ref,
    q_v, ks_v, vs_v, kc_v, vc_v, w_v, len_v, d_v, u_v, ctx_v, part_v, recv_v, fac_v, proj_v, prcv_v, out_v,
    in_sem, w_sem, send_sem, recv_sem, zsend_sem, zrecv_sem, qsend_sem, qrecv_sem, psend_sem, precv_sem, out_sem,
):
    g = lax.axis_index("group")
    t = lax.axis_index("tensor")
    z, quad = g // 4, g % 4
    y, xh = t // 2, t % 2
    dev = lambda gg, yy, xx: (gg, yy * 2 + xx)
    y_up = dev(g, (y + 1) % 4, xh)
    y_down = dev(g, (y + 3) % 4, xh)
    x_peer = dev(g, y, 1 - xh)
    z_peers = [(((z + k) % 8) * 4 + quad, t) for k in range(1, 8)]
    quad_ids = [(quad + k) % 4 for k in range(1, 4)]
    quad_peers = [(z * 4 + k, t) for k in quad_ids]

    contract = (((1,), (1,)), ((), ()))
    barrier = pltpu.get_barrier_semaphore()
    peers = [y_up, y_down, x_peer] + z_peers + quad_peers
    for p in peers:
        pl.semaphore_signal(barrier, inc=1, device_id=p, device_id_type=MESH)

    def fetch(src, dst, sem):
        c = pltpu.make_async_copy(src, dst, sem)
        c.start()
        return c

    loads = []
    w_loads = []

    def load_rows(k, lo, hi):
        rows = pl.ds(lo, hi - lo)
        loads.append([
            fetch(q_ref.at[:, rows, :], q_v.at[:, rows, :], in_sem.at[k, 0]),
            fetch(kc_ref.at[rows], kc_v.at[rows], in_sem.at[k, 1]),
            fetch(vc_ref.at[rows], vc_v.at[rows], in_sem.at[k, 2]),
        ])

    def load_w(i):
        (r, o), h = BLOCKS[i]
        dest = ((y + 4 - r) % 4) * 2 + ((xh + o) % 2)
        cols = pl.ds(pl.multiple_of(dest * COLS + h * HALF, HALF), HALF)
        w_loads.append(fetch(w_ref.at[:, cols], w_v.at[i], w_sem.at[i]))

    fac_loads = [fetch(d_ref, d_v, in_sem.at[0, 3]), fetch(u_ref, u_v, in_sem.at[0, 4])]
    load_rows(0, 0, 16)
    loads[0] += [
        fetch(ks_ref.at[:, 0:GROUP, :], ks_v.at[:, 0:GROUP, :], in_sem.at[1, 3]),
        fetch(vs_ref.at[:, 0:GROUP, :], vs_v.at[:, 0:GROUP, :], in_sem.at[1, 4]),
        fetch(len_ref, len_v, in_sem.at[0, 5]),
    ]
    load_rows(1, 16, GROUP)
    for i in range(6):
        load_w(i)
    def later_loads():
        load_rows(2, GROUP, ROWS)
        loads[2].extend([
            fetch(ks_ref.at[:, GROUP:, :], ks_v.at[:, GROUP:, :], in_sem.at[2, 3]),
            fetch(vs_ref.at[:, GROUP:, :], vs_v.at[:, GROUP:, :], in_sem.at[2, 4]),
        ])
        for i in range(6, len(BLOCKS)):
            load_w(i)

    waited = set()

    def loaded(k):
        if k not in waited:
            waited.add(k)
            for c in loads[k]:
                c.wait()

    def attention(chunk):
        loaded(0 if chunk == 0 else 2)
        row0, rows = ROW0[chunk], CHUNK_ROWS[chunk]
        g0 = row0 // GROUP * GROUP
        ks_c = ks_v[:, g0:g0 + GROUP, :].reshape(STEPS * GROUP, D)
        vs_c = vs_v[:, g0:g0 + GROUP, :].reshape(STEPS * GROUP, D)
        ones = jnp.ones((STEPS * GROUP, D), BF)
        vs_ext = jnp.concatenate([vs_c, ones], axis=1)
        sub = lax.broadcasted_iota(jnp.int32, (8, 2 * D), 0)
        lane = lax.broadcasted_iota(jnp.int32, (8, 2 * D), 1)

        def sixteen(jj, carry):
            r0 = pl.multiple_of(row0 + jj * 16, 16)
            qf = q_v[:, pl.ds(r0, 16), :].astype(F32)
            outs = []
            for part in range(2):
                qb = jnp.concatenate(
                    [
                        qf[s, part * 8:part * 8 + 8, h * D:(h + 1) * D]
                        for s in range(STEPS)
                        for h in range(HEADS)
                    ],
                    axis=0,
                ).astype(BF)
                rp = r0 + part * 8
                k8 = kc_v[pl.ds(rp, 8)].reshape(8 * CACHE, D)
                v8 = vc_v[pl.ds(rp, 8)].reshape(8 * CACHE, D)
                s1 = lax.dot_general(qb, k8, contract, preferred_element_type=F32)
                s2 = lax.dot_general(qb, ks_c, contract, preferred_element_type=F32)
                lens = jnp.zeros((8, 2 * D), jnp.int32)
                for i in range(8):
                    lens = jnp.where(sub == i, len_v[rp + i], lens)
                ok1 = (lane // CACHE == sub) & (lane % CACHE < lens)
                bias1 = jnp.where(ok1, 0.0, NEG).astype(F32)
                sub2, lane2 = sub[:, :D], lane[:, :D]
                mine = lane2 % GROUP == sub2 + (rp - g0)
                bias2 = jnp.stack(
                    [
                        jnp.where(mine & (lane2 // GROUP <= s), 0.0, NEG).astype(F32)
                        for s in range(STEPS)
                    ]
                )
                s1 = s1.reshape(STEPS * HEADS, 8, 2 * D) + bias1[None]
                s2 = s2.reshape(STEPS, HEADS, 8, D) + bias2[:, None]
                s1 = s1.reshape(STEPS * HEADS * 8, 2 * D)
                s2 = s2.reshape(STEPS * HEADS * 8, D)
                top = jnp.maximum(jnp.maximum(s1[:, :D], s1[:, D:]), s2)
                top = jnp.max(top, axis=1, keepdims=True)
                p1 = jnp.exp2((s1 - top) * EXP2_SCALE).astype(BF)
                p2 = jnp.exp2((s2 - top) * EXP2_SCALE).astype(BF)
                v_ext = jnp.concatenate([v8, jnp.ones((8 * CACHE, D), BF)], axis=1)
                acc = jnp.dot(p1, v_ext, preferred_element_type=F32) + jnp.dot(
                    p2, vs_ext, preferred_element_type=F32
                )
                outs.append(acc[:, :D] / acc[:, D:])
            for s in range(STEPS):
                for h in range(HEADS):
                    i = (s * HEADS + h) * 8
                    tile = jnp.concatenate([outs[0][i:i + 8], outs[1][i:i + 8]], axis=0)
                    at = pl.multiple_of(STEPS * row0 + s * rows + jj * 16, 16)
                    ctx_v[pl.ds(at, 16), h * D:(h + 1) * D] = tile.astype(BF)
            return carry

        if chunk == 0:
            for jj in range(rows // 16):
                loaded(jj)
                sixteen(jj, 0)
                if jj == 0:
                    later_loads()
        else:
            lax.fori_loop(0, rows // 16, sixteen, 0)

    def span(chunk):
        return pl.ds(STEPS * ROW0[chunk], STEPS * CHUNK_ROWS[chunk])

    multiplied = set()
    fetched = set()

    def product(chunk, b):
        if (chunk, b) in multiplied:
            return
        multiplied.add((chunk, b))
        i = BLOCK_INDEX[b]
        if i not in fetched:
            fetched.add(i)
            w_loads[i].wait()
        part_v[i, span(chunk), :] = jnp.dot(
            ctx_v[span(chunk), :], w_v[i], preferred_element_type=F32
        ).astype(BF)

    sends = []

    def target_of(node, parent):
        if node[1] != parent[1]:
            return x_peer
        return y_up if (parent[0] - node[0]) % 4 == 1 else y_down

    def edge_copy(chunk, node, h):
        e = EDGE_INDEX[(node, h)]
        parent = trees_of(chunk)[h][node]
        return pltpu.make_async_remote_copy(
            src_ref=part_v.at[BLOCK_INDEX[(node, h)], span(chunk), :],
            dst_ref=recv_v.at[e, span(chunk), :],
            send_sem=send_sem.at[chunk, e],
            recv_sem=recv_sem.at[chunk, e],
            device_id=target_of(node, parent),
            device_id_type=MESH,
        )

    def send(chunk, node, h):
        c = edge_copy(chunk, node, h)
        c.start()
        sends.append(c)

    def gathered(chunk, node, h):
        total = part_v[BLOCK_INDEX[(node, h)], span(chunk), :].astype(F32)
        for kid in children(trees_of(chunk)[h], node):
            edge_copy(chunk, kid, h).wait_recv()
            total = total + recv_v[EDGE_INDEX[(kid, h)], span(chunk), :].astype(F32)
        return total

    def combine(chunk, node, h):
        i = BLOCK_INDEX[(node, h)]
        part_v[i, span(chunk), :] = gathered(chunk, node, h).astype(BF)
        send(chunk, node, h)

    owner = z == t
    z_copies = [
        pltpu.make_async_remote_copy(
            src_ref=fac_v.at[quad], dst_ref=fac_v.at[quad],
            send_sem=zsend_sem.at[k], recv_sem=zrecv_sem.at[0],
            device_id=z_peers[k], device_id_type=MESH,
        )
        for k in range(7)
    ]
    quad_copies = [
        pltpu.make_async_remote_copy(
            src_ref=fac_v.at[quad], dst_ref=fac_v.at[quad],
            send_sem=qsend_sem.at[k], recv_sem=qrecv_sem.at[2 - k],
            device_id=quad_peers[k], device_id_type=MESH,
        )
        for k in range(3)
    ]

    def factors_out():
        for c in fac_loads:
            c.wait()

        @pl.when(owner)
        def _():
            fac_v[quad, 0:D, :] = jnp.concatenate([d_v[:, 0:D], d_v[:, D:2 * D]], axis=0).astype(BF)
            fac_v[quad, D:D + 64, :] = u_v[...].astype(BF)
            for c in z_copies:
                c.start()

    def factors_quad():
        @pl.when(jnp.logical_not(owner))
        def _():
            z_copies[0].wait_recv()

        for c in quad_copies:
            c.start()

    def factors_wait():
        for c in quad_copies:
            c.wait_recv()

    half_m = STEPS * ROWS // 2
    lane_m = lax.broadcasted_iota(jnp.int32, (half_m, D), 1)

    def project():
        halves = []
        for k in range(2):
            lo = jnp.zeros((half_m, D), F32)
            hi = jnp.zeros((half_m, D), F32)
            ctx = ctx_v[k * half_m:(k + 1) * half_m, :]
            for j in range(4):
                f = fac_v[j, 0:D, :]
                lo = lo + lax.dot_general(
                    ctx[:, 2 * j * D:(2 * j + 1) * D], f, contract, preferred_element_type=F32
                )
                hi = hi + lax.dot_general(
                    ctx[:, (2 * j + 1) * D:(2 * j + 2) * D], f, contract, preferred_element_type=F32
                )
            if k == 0:
                halves.append(lo + pltpu.roll(hi, 64, 1))
            else:
                halves.append(hi + pltpu.roll(lo, 64, 1))
        proj_v[0] = jnp.where(lane_m < 64, halves[0], halves[1]).astype(BF)

    y_pair = dev(g, y + 1 - 2 * (y % 2), xh)
    y_flip = dev(g, 3 - y, xh)
    p_copies = [
        pltpu.make_async_remote_copy(
            src_ref=proj_v.at[k], dst_ref=prcv_v.at[k],
            send_sem=psend_sem.at[k], recv_sem=precv_sem.at[k],
            device_id=p, device_id_type=MESH,
        )
        for k, p in enumerate((x_peer, y_pair, y_flip))
    ]

    def proj_step(k):
        p_copies[k].wait_recv()
        proj_v[k + 1] = (proj_v[k].astype(F32) + prcv_v[k].astype(F32)).astype(BF)
        if k < 2:
            p_copies[k + 1].start()

    outs = []

    def finish(chunk):
        rows, m0 = CHUNK_ROWS[chunk], STEPS * ROW0[chunk]
        m = STEPS * rows
        proj = proj_v[3, pl.ds(m0 % half_m, m), :]
        lane = lax.broadcasted_iota(jnp.int32, (m, D), 1)
        keep = lane < 64 if m0 < half_m else lane >= 64
        proj = jnp.where(keep, proj.astype(F32) * ADAPTER_SCALE, 0.0).astype(BF)
        row_span = pl.ds(ROW0[chunk], rows)
        for h in range(2):
            total = gathered(chunk, ROOT, h)
            for j in range(2):
                u = fac_v[2 * h + j, D:D + 64, :]
                low = jnp.dot(proj, jnp.concatenate([u, u], axis=0), preferred_element_type=F32)
                res = (total[:, j * D:(j + 1) * D] + low).astype(BF)
                out_v[:, row_span, h * HALF + j * D:h * HALF + (j + 1) * D] = res.reshape(STEPS, rows, D)
        outs.append(fetch(out_v.at[:, row_span, :], o_ref.at[:, row_span, :], out_sem.at[chunk]))

    ar_steps = 0
    greeted = False
    for kind, v in STEPS_IN_ORDER:
        if kind in "LO" and not greeted:
            greeted = True
            pl.semaphore_wait(barrier, len(peers))
        if kind == "A":
            attention(v[0])
        elif kind == "O":
            factors_out()
        elif kind in "LMC":
            chunk, node, h = v[0], (v[1], v[2]), v[3]
            product(chunk, (node, h))
            if kind == "L":
                send(chunk, node, h)
            elif kind == "C":
                combine(chunk, node, h)
        elif kind == "F":
            for h in (0, 1):
                product(v[0], (ROOT, h))
            finish(v[0])
        elif kind == "Q":
            factors_quad()
        elif kind == "P":
            factors_wait()
            project()
            p_copies[0].start()
        else:
            proj_step(ar_steps)
            ar_steps += 1

    for c in sends:
        c.wait_send()

    @pl.when(owner)
    def _():
        for c in z_copies:
            c.wait_send()

    for c in quad_copies + p_copies:
        c.wait_send()
    for c in outs:
        c.wait()


def body(q, ks, vs, kc, vc, lengths, w, d, u):
    hbm = pl.BlockSpec(memory_space=pltpu.HBM)
    dma = pltpu.SemaphoreType.DMA
    return pl.pallas_call(
        kernel,
        out_shape=jax.ShapeDtypeStruct((STEPS, ROWS, COLS), BF),
        in_specs=[hbm] * 9,
        out_specs=hbm,
        scratch_shapes=[
            pltpu.VMEM((STEPS, ROWS, WIDTH), BF),
            pltpu.VMEM((STEPS, ROWS, D), BF),
            pltpu.VMEM((STEPS, ROWS, D), BF),
            pltpu.VMEM((ROWS, CACHE, D), BF),
            pltpu.VMEM((ROWS, CACHE, D), BF),
            pltpu.VMEM((16, WIDTH, HALF), BF),
            pltpu.SMEM((ROWS,), jnp.int32),
            pltpu.VMEM((64, 256), F32),
            pltpu.VMEM((64, 128), F32),
            pltpu.VMEM((STEPS * ROWS, WIDTH), BF),
            pltpu.VMEM((16, STEPS * ROWS, HALF), BF),
            pltpu.VMEM((14, STEPS * ROWS, HALF), BF),
            pltpu.VMEM((4, D + 64, D), BF),
            pltpu.VMEM((4, STEPS * ROWS // 2, D), BF),
            pltpu.VMEM((3, STEPS * ROWS // 2, D), BF),
            pltpu.VMEM((STEPS, ROWS, COLS), BF),
            dma((3, 6)),
            dma((16,)),
            dma((CHUNKS, 14)),
            dma((CHUNKS, 14)),
            dma((7,)),
            dma((1,)),
            dma((3,)),
            dma((3,)),
            dma((3,)),
            dma((3,)),
            dma((CHUNKS,)),
        ],
        compiler_params=pltpu.CompilerParams(
            collective_id=1, has_side_effects=True, vmem_limit_bytes=64 << 20
        ),
        cost_estimate=pl.CostEstimate(
            flops=2 * 512 * 1024 * 4200, bytes_accessed=13 << 20, transcendentals=1 << 20
        ),
        name="attend_project_reduce",
    )(q, ks, vs, kc, vc, lengths, w, d.T, u)


def solution(mesh):
    return jax.shard_map(
        body,
        mesh=mesh,
        in_specs=(
            P(None, "group", "tensor"),
            P(None, "group", "tensor"),
            P(None, "group", "tensor"),
            P("group", None, "tensor"),
            P("group", None, "tensor"),
            P("group"),
            P("tensor", None),
            P("group", None),
            P(None, "group"),
        ),
        out_specs=P(None, "group", "tensor"),
        check_vma=False,
    )
```

time: 63.7 us -> 47.1 us (0.74); the launches traced: 62.5 us -> 47 us
  Pallas kernels: 53.8 us -> 45.1 us
  local copies, waits for them, and re-layouts: 8.62 us -> 1.87 us
    pallas_call x1, Pallas kernels: 53.8 us -> 45.1 us  [body(): pl.pallas_call(kernel, out_shape=jax.ShapeDtypeStruct((STEPS, ROWS, COLS)...]
    unnamed x16 -> x1, local copies, waits for them, and re-layouts: 8.62 us -> 1.87 us
where the time goes in v2:
time: 47.1 us; the launch traced here: 47 us
  Pallas kernels  45.1 us (96%)
  local copies, waits for them, and re-layouts  1.87 us (4%)
    pallas_call x1, Pallas kernels, body(): pl.pallas_call(kernel, out_shape=jax.ShapeDtypeStruct((STEPS, ROWS, COLS)...  45.1 us
    unnamed x1, local copies, waits for them, and re-layouts  1.87 us

profile of v2, /device:TPU:2, one launch (start us, length us, event | category | flops | bytes accessed | tf_op | source)
XLA Modules:
  0.0 47.0 jit_solution(8040536006371027397)
XLA Ops:
  0.0 45.1 %attend_project_reduce.1 = bf16[4,128,512]{2,1,0:T(8,128)(2,1)} custom-call(bf16[4,128,1024]{2,1,0:T(8,128)(2,1)} %q_ref.1, bf16[4,128,128]{2,1,0:T(8,128)(2,1)} %ks_ref.1, bf16[4,128,128]{2,1,0:T(8,128)(2,1)} %vs_ref.1, bf16[128,32,128]{2,1,0:T(8,128)(2,1)} %kc_ref.1, bf16[128,32,128]{2,1,0:T(8,128)(2,1)} %vc_ref.1, s32[128]{0:T(128)} %len_ref.1, ...), custom_call_target="tpu_custom_call" | custom-call | flops 4404019200 | bytes 13631488 | tf_op jit(solution)/shard_map/attend_project_reduce/pallas_call | solution.py:435
  45.1 1.9 %copy.11 = bf16[4,128,512]{2,1,0:T(8,128)(2,1)} copy(bf16[4,128,512]{2,1,0:T(8,128)(2,1)} %attend_project_reduce.1) | data formatting | bytes 1048576

commit v3 on v2

--- a/solution.py
+++ b/solution.py
@@ -57,13 +57,13 @@
 
 ORDER = (
     "A0", "O", "L0210", "L0211", "L0110", "L0310", "L0111", "L0311", "A1", "L1210", "L1211", "L1200", "L1310",
-    "L1201", "L1111", "L1300", "C0200", "C0010", "L1101", "C0011", "A2", "C0201", "C0300", "C1110", "C1311",
-    "L2210", "C1100", "Q", "L2211", "L2110", "C0101", "L2310", "L2111", "L2311", "M0100", "M0301", "C1301",
-    "M0000", "M0001", "M1010", "M1011", "M1000", "M1001", "M2200", "M2201", "C0100", "M2100", "M2300", "M2010",
-    "M2101", "M2301", "M2011", "M2000", "M2001", "A3", "C0301", "C1010", "C2200", "L3210", "L3211", "L3200",
-    "L3110", "L3201", "L3311", "M3310", "P", "C1011", "M3111", "M3100", "M3300", "M3010", "M3101", "M3301",
-    "C2201", "C2010", "C2011", "M3011", "M3000", "M3001", "C2300", "C2101", "C2100", "C3310", "R", "C3111",
-    "C3301", "C3100", "C3011", "C3010", "C2301", "C3300", "R", "C3101", "R", "F0", "F1", "F2", "F3",
+    "L1201", "L1111", "L1300", "C0200", "C0010", "L1101", "C0011", "A2", "Q", "C0201", "C0300", "C1110", "C1311",
+    "L2210", "C1100", "L2211", "L2110", "C0101", "L2310", "L2111", "L2311", "M0100", "M0301", "C1301", "M0000",
+    "M0001", "M1010", "M1011", "M1000", "M1001", "M2200", "M2201", "C0100", "M2100", "M2300", "M2010", "M2101",
+    "M2301", "M2011", "M2000", "M2001", "A3", "C0301", "C1010", "C2200", "L3210", "L3211", "L3200", "L3110",
+    "L3201", "L3311", "M3310", "C1011", "M3111", "M3100", "M3300", "M3010", "M3101", "M3301", "P", "C2201",
+    "C2010", "C2011", "M3011", "M3000", "M3001", "C2300", "C2101", "C2100", "C3310", "R", "C3111", "C3301",
+    "C3100", "C3011", "C3010", "C2301", "C3300", "R", "C3101", "R", "F0", "F1", "F2", "F3",
 )
 STEPS_IN_ORDER = [(w[0], tuple(int(x) for x in w[1:])) for w in ORDER]
 
@@ -88,8 +88,8 @@
 
 def kernel(
     q_ref, ks_ref, vs_ref, kc_ref, vc_ref, len_ref, w_ref, d_ref, u_ref, o_ref,
-    q_v, ks_v, vs_v, kc_v, vc_v, w_v, len_v, d_v, u_v, ctx_v, part_v, recv_v, fac_v, proj_v, prcv_v, out_v,
-    in_sem, w_sem, send_sem, recv_sem, zsend_sem, zrecv_sem, qsend_sem, qrecv_sem, psend_sem, precv_sem, out_sem,
+    q_v, ks_v, vs_v, kc_v, vc_v, w_v, len_v, d_v, u_v, ctx_v, part_v, recv_v, fac_v, proj_v, prcv_v,
+    in_sem, w_sem, send_sem, recv_sem, zsend_sem, zrecv_sem, qsend_sem, qrecv_sem, psend_sem, precv_sem,
 ):
     g = lax.axis_index("group")
     t = lax.axis_index("tensor")
@@ -285,21 +285,28 @@
         send(chunk, node, h)
 
     owner = z == t
+    parts = [fac_v.at[quad, pl.ds(0, D), :], fac_v.at[quad, pl.ds(D, 64), :]]
     z_copies = [
-        pltpu.make_async_remote_copy(
-            src_ref=fac_v.at[quad], dst_ref=fac_v.at[quad],
-            send_sem=zsend_sem.at[k], recv_sem=zrecv_sem.at[0],
-            device_id=z_peers[k], device_id_type=MESH,
-        )
-        for k in range(7)
+        [
+            pltpu.make_async_remote_copy(
+                src_ref=part, dst_ref=part,
+                send_sem=zsend_sem.at[k, i], recv_sem=zrecv_sem.at[i],
+                device_id=z_peers[k], device_id_type=MESH,
+            )
+            for k in range(7)
+        ]
+        for i, part in enumerate(parts)
     ]
     quad_copies = [
-        pltpu.make_async_remote_copy(
-            src_ref=fac_v.at[quad], dst_ref=fac_v.at[quad],
-            send_sem=qsend_sem.at[k], recv_sem=qrecv_sem.at[2 - k],
-            device_id=quad_peers[k], device_id_type=MESH,
-        )
-        for k in range(3)
+        [
+            pltpu.make_async_remote_copy(
+                src_ref=part, dst_ref=part,
+                send_sem=qsend_sem.at[k, i], recv_sem=qrecv_sem.at[2 - k, i],
+                device_id=quad_peers[k], device_id_type=MESH,
+            )
+            for k in range(3)
+        ]
+        for i, part in enumerate(parts)
     ]
 
     def factors_out():
@@ -310,19 +317,19 @@
         def _():
             fac_v[quad, 0:D, :] = jnp.concatenate([d_v[:, 0:D], d_v[:, D:2 * D]], axis=0).astype(BF)
             fac_v[quad, D:D + 64, :] = u_v[...].astype(BF)
-            for c in z_copies:
+            for c in z_copies[0] + z_copies[1]:
                 c.start()
 
-    def factors_quad():
+    def factors_quad(i):
         @pl.when(jnp.logical_not(owner))
         def _():
-            z_copies[0].wait_recv()
-
-        for c in quad_copies:
+            z_copies[i][0].wait_recv()
+
+        for c in quad_copies[i]:
             c.start()
 
-    def factors_wait():
-        for c in quad_copies:
+    def factors_wait(i):
+        for c in quad_copies[i]:
             c.wait_recv()
 
     half_m = STEPS * ROWS // 2
@@ -365,8 +372,6 @@
         if k < 2:
             p_copies[k + 1].start()
 
-    outs = []
-
     def finish(chunk):
         rows, m0 = CHUNK_ROWS[chunk], STEPS * ROW0[chunk]
         m = STEPS * rows
@@ -381,10 +386,9 @@
                 u = fac_v[2 * h + j, D:D + 64, :]
                 low = jnp.dot(proj, jnp.concatenate([u, u], axis=0), preferred_element_type=F32)
                 res = (total[:, j * D:(j + 1) * D] + low).astype(BF)
-                out_v[:, row_span, h * HALF + j * D:h * HALF + (j + 1) * D] = res.reshape(STEPS, rows, D)
-        outs.append(fetch(out_v.at[:, row_span, :], o_ref.at[:, row_span, :], out_sem.at[chunk]))
-
-    ar_steps = 0
+                o_ref[:, row_span, h * HALF + j * D:h * HALF + (j + 1) * D] = res.reshape(STEPS, rows, D)
+
+    ar_steps = finished = 0
     greeted = False
     for kind, v in STEPS_IN_ORDER:
         if kind in "LO" and not greeted:
@@ -404,13 +408,17 @@
         elif kind == "F":
             for h in (0, 1):
                 product(v[0], (ROOT, h))
+            if not finished:
+                factors_wait(1)
+            finished += 1
             finish(v[0])
         elif kind == "Q":
-            factors_quad()
+            factors_quad(0)
         elif kind == "P":
-            factors_wait()
+            factors_wait(0)
             project()
             p_copies[0].start()
+            factors_quad(1)
         else:
             proj_step(ar_steps)
             ar_steps += 1
@@ -420,13 +428,11 @@
 
     @pl.when(owner)
     def _():
-        for c in z_copies:
+        for c in z_copies[0] + z_copies[1]:
             c.wait_send()
 
-    for c in quad_copies + p_copies:
+    for c in quad_copies[0] + quad_copies[1] + p_copies:
         c.wait_send()
-    for c in outs:
-        c.wait()
 
 
 def body(q, ks, vs, kc, vc, lengths, w, d, u):
@@ -434,9 +440,9 @@
     dma = pltpu.SemaphoreType.DMA
     return pl.pallas_call(
         kernel,
-        out_shape=jax.ShapeDtypeStruct((STEPS, ROWS, COLS), BF),
+        out_shape=pltpu.VMEM((STEPS, ROWS, COLS), BF),
         in_specs=[hbm] * 9,
-        out_specs=hbm,
+        out_specs=pl.BlockSpec(memory_space=pltpu.VMEM),
         scratch_shapes=[
             pltpu.VMEM((STEPS, ROWS, WIDTH), BF),
             pltpu.VMEM((STEPS, ROWS, D), BF),
@@ -453,21 +459,19 @@
             pltpu.VMEM((4, D + 64, D), BF),
             pltpu.VMEM((4, STEPS * ROWS // 2, D), BF),
             pltpu.VMEM((3, STEPS * ROWS // 2, D), BF),
-            pltpu.VMEM((STEPS, ROWS, COLS), BF),
             dma((3, 6)),
             dma((16,)),
             dma((CHUNKS, 14)),
             dma((CHUNKS, 14)),
-            dma((7,)),
-            dma((1,)),
+            dma((7, 2)),
+            dma((2,)),
+            dma((3, 2)),
+            dma((3, 2)),
             dma((3,)),
             dma((3,)),
-            dma((3,)),
-            dma((3,)),
-            dma((CHUNKS,)),
         ],
         compiler_params=pltpu.CompilerParams(
-            collective_id=1, has_side_effects=True, vmem_limit_bytes=64 << 20
+            collective_id=1, has_side_effects=True, vmem_limit_bytes=54 << 20
         ),
         cost_estimate=pl.CostEstimate(
             flops=2 * 512 * 1024 * 4200, bytes_accessed=13 << 20, transcendentals=1 << 20

time: 47.1 us -> 45.3 us (0.962)
  local copies, waits for them, and re-layouts: 1.87 us -> 0.8 us
  Pallas kernels: 45.1 us -> 44.4 us
    unnamed x1, local copies, waits for them, and re-layouts: 1.87 us -> 0.8 us
    pallas_call x1, Pallas kernels: 45.1 us -> 44.4 us  [body(): pl.pallas_call(kernel, out_shape=pltpu.VMEM((STEPS, ROWS, COLS), BF), in_...]
where the time goes in v3:
time: 45.3 us; the launch traced here: 45.2 us
  Pallas kernels  44.4 us (98%)
  local copies, waits for them, and re-layouts  0.8 us (2%)
    pallas_call x1, Pallas kernels, body(): pl.pallas_call(kernel, out_shape=pltpu.VMEM((STEPS, ROWS, COLS), BF), in_...  44.4 us

profile of v3, /device:TPU:2, one launch (start us, length us, event | category | flops | bytes accessed | tf_op | source)
XLA Modules:
  0.0 45.2 jit_solution(2518977530311533205)
XLA Ops:
  0.0 44.4 %attend_project_reduce.1 = bf16[4,128,512]{2,1,0:T(8,128)(2,1)S(1)} custom-call(bf16[4,128,1024]{2,1,0:T(8,128)(2,1)} %q_ref.1, bf16[4,128,128]{2,1,0:T(8,128)(2,1)} %ks_ref.1, bf16[4,128,128]{2,1,0:T(8,128)(2,1)} %vs_ref.1, bf16[128,32,128]{2,1,0:T(8,128)(2,1)} %kc_ref.1, bf16[128,32,128]{2,1,0:T(8,128)(2,1)} %vc_ref.1, s32[128]{0:T(128)} %len_ref.1, ...), custom_call_target="tpu_custom_call" | custom-call | flops 4404019200 | bytes 13631488 | tf_op jit(solution)/shard_map/attend_project_reduce/pallas_call | solution.py:441
  44.4 0.8 %copy.11 = bf16[4,128,512]{2,1,0:T(8,128)(2,1)} copy(bf16[4,128,512]{2,1,0:T(8,128)(2,1)S(1)} %attend_project_reduce.1) | data formatting | bytes 1048576

commit v4 on v3

--- a/solution.py
+++ b/solution.py
@@ -57,13 +57,13 @@
 
 ORDER = (
     "A0", "O", "L0210", "L0211", "L0110", "L0310", "L0111", "L0311", "A1", "L1210", "L1211", "L1200", "L1310",
-    "L1201", "L1111", "L1300", "C0200", "C0010", "L1101", "C0011", "A2", "Q", "C0201", "C0300", "C1110", "C1311",
-    "L2210", "C1100", "L2211", "L2110", "C0101", "L2310", "L2111", "L2311", "M0100", "M0301", "C1301", "M0000",
-    "M0001", "M1010", "M1011", "M1000", "M1001", "M2200", "M2201", "C0100", "M2100", "M2300", "M2010", "M2101",
-    "M2301", "M2011", "M2000", "M2001", "A3", "C0301", "C1010", "C2200", "L3210", "L3211", "L3200", "L3110",
-    "L3201", "L3311", "M3310", "C1011", "M3111", "M3100", "M3300", "M3010", "M3101", "M3301", "P", "C2201",
-    "C2010", "C2011", "M3011", "M3000", "M3001", "C2300", "C2101", "C2100", "C3310", "R", "C3111", "C3301",
-    "C3100", "C3011", "C3010", "C2301", "C3300", "R", "C3101", "R", "F0", "F1", "F2", "F3",
+    "L1201", "L1111", "L1300", "C0200", "C0010", "L1101", "C0011", "A2", "C0201", "C0300", "C1110", "C1311",
+    "L2210", "C1100", "Q", "L2211", "L2110", "C0101", "L2310", "L2111", "L2311", "M0100", "M0301", "C1301",
+    "M0000", "M0001", "M1010", "M1011", "M1000", "M1001", "M2200", "M2201", "C0100", "M2100", "M2300", "M2010",
+    "M2101", "M2301", "M2011", "M2000", "M2001", "A3", "C0301", "C1010", "C2200", "L3210", "L3211", "L3200",
+    "L3110", "L3201", "L3311", "M3310", "C1011", "M3111", "M3100", "M3300", "M3010", "M3101", "M3301", "C2201",
+    "P", "C2010", "C2011", "M3011", "M3000", "M3001", "C2300", "C2101", "C2100", "C3310", "R", "C3111", "C3301",
+    "C3100", "C3011", "C3010", "R", "C2301", "C3300", "C3101", "R", "F0", "F1", "F2", "F3",
 )
 STEPS_IN_ORDER = [(w[0], tuple(int(x) for x in w[1:])) for w in ORDER]
 

time: 45.3 us -> 45 us (level)
  Pallas kernels: 44.4 us -> 43.8 us
    pallas_call x1, Pallas kernels: 44.4 us -> 43.8 us  [body(): pl.pallas_call(kernel, out_shape=pltpu.VMEM((STEPS, ROWS, COLS), BF), in_...]
where the time goes in v4:
time: 45 us; the launch traced here: 44.6 us
  Pallas kernels  43.8 us (97%)
  local copies, waits for them, and re-layouts  0.8 us (2%)
    pallas_call x1, Pallas kernels, body(): pl.pallas_call(kernel, out_shape=pltpu.VMEM((STEPS, ROWS, COLS), BF), in_...  43.8 us

profile of v4, /device:TPU:2, one launch (start us, length us, event | category | flops | bytes accessed | tf_op | source)
XLA Modules:
  0.0 44.6 jit_solution(13154407580496584624)
XLA Ops:
  0.0 43.8 %attend_project_reduce.1 = bf16[4,128,512]{2,1,0:T(8,128)(2,1)S(1)} custom-call(bf16[4,128,1024]{2,1,0:T(8,128)(2,1)} %q_ref.1, bf16[4,128,128]{2,1,0:T(8,128)(2,1)} %ks_ref.1, bf16[4,128,128]{2,1,0:T(8,128)(2,1)} %vs_ref.1, bf16[128,32,128]{2,1,0:T(8,128)(2,1)} %kc_ref.1, bf16[128,32,128]{2,1,0:T(8,128)(2,1)} %vc_ref.1, s32[128]{0:T(128)} %len_ref.1, ...), custom_call_target="tpu_custom_call" | custom-call | flops 4404019200 | bytes 13631488 | tf_op jit(solution)/shard_map/attend_project_reduce/pallas_call | solution.py:441
  43.8 0.8 %copy.11 = bf16[4,128,512]{2,1,0:T(8,128)(2,1)} copy(bf16[4,128,512]{2,1,0:T(8,128)(2,1)S(1)} %attend_project_reduce.1) | data formatting | bytes 1048576
